TPU v7x, 32 devices: a whole 2x2x4 slice. The times are simulated.
32 devices in a mesh: space: 16 (over z, x, core), scen: 2 (over y).
Axes of the slice: x: 2, y: 2, z: 4, core: 2. Of those that a mesh axis runs over, the one named last changes fastest.
Arguments:
- concentration: float32 [2, 8, 6, 384, 384], P('scen', None, None, 'space'), may hold values from -6 to 6
- emissions: float32 [2, 6, 384, 384], P('scen', None, 'space'), may hold values from -3 to 3
- courant: float32 [2, 8, 6, 384, 384], P(None, None, None, 'space'), may hold values from -0.9 to 0.9
- tile_source: int32 [8640], P('space'), may hold values from 0 to 431, as said below
- tile_target: int32 [8640], P('space'), may hold values from 0 to 511, as said below
- intersection: bfloat16 [8640, 128, 128], P('space'), may hold values from 0 to 0.0625
Outputs:
- transported: float32 [2, 8, 6, 384, 384], P('scen', None, None, 'space')
- regridded: float32 [2, 8, 512, 128], P('scen', None, 'space')
- ensemble_moments: float32 [2, 8, 512, 128], P(None, None, 'space')
Inputs may be any that keep to these rules, and one draw needn't show every extreme that they name: `tile_source`: every source block of a row band is named by at least one of the band's tiles. `tile_target`: latitude band b holds target blocks b * 32 to (b+1) * 32 - 1. The 540 tiles of one row band name at most 67 blocks of any one latitude band and at least 31 of every latitude band but one, which receives exactly 67 tiles from every row band. Every target block is named by some tile.
All inputs are finite; a program needn't handle non-finite values.
Results may differ from a plain program's by a relative error of at most 0.0027.
Values sent between devices are 32-bit elements; how exact they have to be, the bound alone decides.
A program may use at most 128 MiB of HBM per device.

v0:
```python
import functools

import jax
import jax.numpy as jnp
from jax import lax
from jax.experimental import pallas as pl
from jax.experimental.pallas import tpu as pltpu
from jax.sharding import PartitionSpec as P

TGT_DEV = 32


MESH = pl.DeviceIdType.MESH
HIGHEST = lax.Precision.HIGHEST


def parabola_sweep(values, courant_faces, axis):
    count = values.shape[axis]
    behind = pltpu.roll(values, 1, axis)
    edges = (7.0 / 12.0) * (behind + values) - (1.0 / 12.0) * (
        pltpu.roll(values, 2, axis) + pltpu.roll(values, count - 1, axis)
    )
    forward = courant_faces >= 0.0
    speed = jnp.abs(courant_faces)
    far = jnp.where(forward, pltpu.roll(edges, 1, axis), pltpu.roll(edges, count - 1, axis))
    centre = jnp.where(forward, behind, values)
    curvature = 6.0 * centre - 3.0 * (edges + far)
    flux = courant_faces * (
        edges + 0.5 * speed * ((far - edges) + (1.0 - (2.0 / 3.0) * speed) * curvature)
    )
    return values - (pltpu.roll(flux, count - 1, axis) - flux)


def transport_kernel(
    bands,
    conc_ref,
    emis_ref,
    wind_ref,
    out_ref,
    block_ref,
    tracer,
    east,
    north,
    edge_pack,
    edge_turned,
    top_edge,
    low_edge,
    even_columns,
    odd_columns,
    gathered,
    turned,
    rows_up,
    rows_down,
    from_south,
    from_north,
    edge_send,
    edge_recv,
    column_send,
    column_recv,
    row_send,
    row_recv,
):
    me = lax.axis_index("space")
    top = bands - 1
    levels, rows, width = conc_ref.shape[1], conc_ref.shape[3], conc_ref.shape[4]
    tall, full = tracer.shape[2], tracer.shape[3]
    held = edge_turned.shape[2]
    slots = edge_pack.shape[1]
    at_top, at_low = me == top, me == 0

    barrier = pltpu.get_barrier_semaphore()

    def greet(band, carry):
        @pl.when(band != me)
        def _():
            pl.semaphore_signal(barrier, inc=1, device_id={"space": band}, device_id_type=MESH)

        return carry

    lax.fori_loop(0, bands, greet, 0)

    across = lax.broadcasted_iota(jnp.int32, (width, width), 0) + lax.broadcasted_iota(
        jnp.int32, (width, width), 1
    )
    mirror = (across == width - 1).astype(jnp.float32)
    lane = lax.broadcasted_iota(jnp.int32, (held, 128), 1)

    def load(level, carry):
        extra = jnp.where(level == 0, 1.0, 0.0)
        for face in range(6):
            tracer[level, face, 0:rows, 0:width] = (
                conc_ref[0, level, face] + extra * emis_ref[0, face]
            )
        return carry

    lax.fori_loop(0, levels, load, 0)
    even_columns[...] = jnp.zeros_like(even_columns)
    odd_columns[...] = jnp.zeros_like(odd_columns)
    edge_pack[...] = jnp.zeros_like(edge_pack)
    edge_turned[...] = jnp.zeros_like(edge_turned)

    def edge_copy(step, band, target):
        is_top = target is top_edge
        return pltpu.make_async_remote_copy(
            src_ref=edge_turned.at[step, band],
            dst_ref=target.at[step],
            send_sem=edge_send.at[step, band],
            recv_sem=edge_recv.at[step, 0 if is_top else 1],
            device_id={"space": band},
            device_id_type=MESH,
        )

    def column_copy(step, source, band, to_top):
        return pltpu.make_async_remote_copy(
            src_ref=source.at[step],
            dst_ref=gathered.at[step, band],
            send_sem=column_send.at[step, 0 if to_top else 1],
            recv_sem=column_recv.at[step, band],
            device_id={"space": top if to_top else 0},
            device_id_type=MESH,
        )

    def row_copies(step):
        upward = pltpu.make_async_remote_copy(
            src_ref=rows_up.at[step],
            dst_ref=from_south.at[step],
            send_sem=row_send.at[step, 0],
            recv_sem=row_recv.at[step, 0],
            device_id={"space": lax.rem(me + 1, bands)},
            device_id_type=MESH,
        )
        downward = pltpu.make_async_remote_copy(
            src_ref=rows_down.at[step],
            dst_ref=from_north.at[step],
            send_sem=row_send.at[step, 1],
            recv_sem=row_recv.at[step, 1],
            device_id={"space": lax.rem(me + bands - 1, bands)},
            device_id_type=MESH,
        )
        return upward, downward

    def each_other(action):
        def body(band, carry):
            @pl.when(band != me)
            def _():
                action(band)

            return carry

        lax.fori_loop(0, bands, body, 0)

    for step in range(2):
        for is_top, own, target in ((True, at_top, top_edge), (False, at_low, low_edge)):

            @pl.when(own)
            def _(step=step, is_top=is_top, target=target):
                def pack(level, carry):
                    for pair in range(3):
                        face = 2 * pair if is_top else 2 * pair + 1
                        first = rows - 3 if is_top else 0
                        edge_pack[level, 3 * pair : 3 * pair + 3, :] = tracer[
                            level, face, first : first + 3, 0:width
                        ]
                        if step == 0:
                            row = rows - 1 if is_top else 0
                            edge_pack[level, 9 + pair : 10 + pair, :] = wind_ref[
                                1, level, face, row : row + 1, :
                            ]
                    return carry

                lax.fori_loop(0, levels, pack, 0)
                flat = edge_pack[...].reshape(levels * slots, width)
                result = lax.dot_general(
                    mirror,
                    flat,
                    (((1,), (1,)), ((), ())),
                    precision=HIGHEST,
                    preferred_element_type=jnp.float32,
                )
                for band in range(bands):
                    edge_turned[step, band, 0:rows, :] = result[band * rows : (band + 1) * rows]

        if step == 0:
            pl.semaphore_wait(barrier, bands - 1)
        for own, target in ((at_top, top_edge), (at_low, low_edge)):

            @pl.when(own)
            def _(step=step, target=target):
                each_other(lambda band: edge_copy(step, band, target).start())
                target[step] = edge_turned[step, me]

            @pl.when(jnp.logical_not(own))
            def _(step=step, target=target):
                edge_copy(step, me, target).wait_recv()

        def sweep_east(level, carry, step=step):
            top_part = top_edge[step]
            low_part = low_edge[step]

            def moved(part, place, lane_to):
                shift = lax.rem(lane_to - place + 256, 128)
                return pltpu.roll(part, shift, 1)

            halves = lane[0:rows] >= 64
            for face in range(6):
                if face % 2 == 0:
                    base = level * slots + 3 * (((face - 2) % 6) // 2)
                    west_cells = moved(top_part, base, 125)[0:rows]
                    east_cells = tracer[level, (face + 1) % 6, 0:rows, 0:128]
                else:
                    west_cells = tracer[level, face - 1, 0:rows, width - 128 : width]
                    base = level * slots + 3 * (((face + 2) % 6) // 2)
                    east_cells = moved(low_part, base, 0)[0:rows]
                tracer[level, face, 0:rows, width:full] = jnp.where(
                    halves, west_cells, east_cells
                )
                if step == 0:
                    if face % 2 == 0:
                        base = level * slots + 9 + ((face - 2) % 6) // 2
                        west_wind = moved(top_part, base, 127)[0:rows]
                        east_wind = wind_ref[0, level, (face + 1) % 6, :, 0:128]
                    else:
                        west_wind = wind_ref[0, level, face - 1, :, width - 128 : width]
                        base = level * slots + 9 + ((face + 2) % 6) // 2
                        east_wind = moved(low_part, base, 0)[0:rows]
                    east[level, face, 0:rows, 0:width] = wind_ref[0, level, face]
                    east[level, face, 0:rows, width:full] = jnp.where(
                        halves, west_wind, east_wind
                    )
                    cells = east[level, face]
                    east[level, face] = 0.5 * (pltpu.roll(cells, 1, 1) + cells)
            for face in range(6):
                swept = parabola_sweep(tracer[level, face, 0:held, :], east[level, face], 1)
                tracer[level, face, 0:rows, 0:width] = swept[0:rows, 0:width]
                rows_down[step, level, 3 * face : 3 * face + 3, :] = swept[0:3, 0:width]
                rows_up[step, level, 3 * face : 3 * face + 3, :] = swept[rows - 3 : rows, 0:width]
                base = level * slots + 3 * (face // 2)
                if face % 2 == 0:
                    edge = jnp.where(lane < 3, swept[:, 0:128], 0.0)
                    even_columns[step] = even_columns[step] + moved(edge, 0, base)
                else:
                    edge = jnp.where(lane >= 125, swept[:, width - 128 : width], 0.0)
                    odd_columns[step] = odd_columns[step] + moved(edge, 125, base)
                if step == 0:
                    rows_down[step, level, 18 + face : 19 + face, :] = wind_ref[1, level, face, 0:1, :]
                    rows_up[step, level, 18 + face : 19 + face, :] = wind_ref[
                        1, level, face, rows - 1 : rows, :
                    ]
                    base = level * slots + 9 + face // 2
                    some = lane[0:rows]
                    if face % 2 == 0:
                        edge = jnp.where(some < 1, wind_ref[0, level, face, :, 0:128], 0.0)
                        even_columns[step, 0:rows] = even_columns[step, 0:rows] + moved(
                            edge, 0, base
                        )
                    else:
                        edge = jnp.where(
                            some >= 127, wind_ref[0, level, face, :, width - 128 : width], 0.0
                        )
                        odd_columns[step, 0:rows] = odd_columns[step, 0:rows] + moved(
                            edge, 127, base
                        )
            return carry

        lax.fori_loop(0, levels, sweep_east, 0)

        upward, downward = row_copies(step)
        upward.start()
        downward.start()
        for own, source, to_top in ((at_top, even_columns, True), (at_low, odd_columns, False)):

            @pl.when(jnp.logical_not(own))
            def _(step=step, source=source, to_top=to_top):
                column_copy(step, source, me, to_top).start()

            @pl.when(own)
            def _(step=step, source=source, to_top=to_top):
                gathered[step, me] = source[step]
                each_other(lambda band: column_copy(step, source, band, to_top).wait_recv())
                strips = [gathered[step, band, 0:rows, :] for band in range(bands)]
                columns = jnp.concatenate(strips, 0)
                result = jnp.dot(
                    jnp.transpose(columns),
                    mirror,
                    precision=HIGHEST,
                    preferred_element_type=jnp.float32,
                )
                turned[...] = result.reshape(levels, slots, width)

        upward.wait_recv()
        downward.wait_recv()

        def sweep_north(level, carry, step=step):
            for face in range(6):
                north_face, south_face = face, face
                if face % 2 == 0:
                    pair = ((face + 2) % 6) // 2
                    beyond = from_north[step, level, 3 * face : 3 * face + 3, :]
                    beyond = jnp.where(at_top, turned[level, 3 * pair : 3 * pair + 3, :], beyond)
                    other = (face - 1) % 6
                    before = jnp.where(
                        at_low,
                        from_south[step, level, 3 * other : 3 * other + 3, :],
                        from_south[step, level, 3 * face : 3 * face + 3, :],
                    )
                else:
                    other = (face + 1) % 6
                    beyond = jnp.where(
                        at_top,
                        from_north[step, level, 3 * other : 3 * other + 3, :],
                        from_north[step, level, 3 * face : 3 * face + 3, :],
                    )
                    pair = ((face - 2) % 6) // 2
                    before = from_south[step, level, 3 * face : 3 * face + 3, :]
                    before = jnp.where(at_low, turned[level, 3 * pair : 3 * pair + 3, :], before)
                tracer[level, face, rows : rows + 3, 0:width] = beyond
                tracer[level, face, tall - 3 : tall, 0:width] = before
                if step == 0:
                    own_row = 18 + face
                    other_row = 18 + other
                    turned_wind = turned[level, 9 + pair : 10 + pair, :]
                    beyond = from_north[step, level, own_row : own_row + 1, :]
                    before = from_south[step, level, own_row : own_row + 1, :]
                    if face % 2 == 0:
                        beyond = jnp.where(at_top, turned_wind, beyond)
                        before = jnp.where(
                            at_low, from_south[step, level, other_row : other_row + 1, :], before
                        )
                    else:
                        beyond = jnp.where(
                            at_top, from_north[step, level, other_row : other_row + 1, :], beyond
                        )
                        before = jnp.where(at_low, turned_wind, before)
                    north[level, face, 0:rows, :] = wind_ref[1, level, face]
                    north[level, face, rows : rows + 1, :] = beyond
                    north[level, face, tall - 1 : tall, :] = before
                    cells = north[level, face]
                    north[level, face] = 0.5 * (pltpu.roll(cells, 1, 0) + cells)
                swept = parabola_sweep(tracer[level, face, :, 0:width], north[level, face], 0)
                if step == 0:
                    tracer[level, face, 0:rows, 0:width] = swept[0:rows]
                else:
                    out_ref[0, level, face] = swept[0:rows]
                    parts = width // 128
                    for part in range(parts):
                        start = face * rows * parts * levels + part * levels + level
                        block_ref[pl.ds(start, rows, stride=parts * levels), :] = swept[
                            0:rows, part * 128 : (part + 1) * 128
                        ]
            return carry

        lax.fori_loop(0, levels, sweep_north, 0)

    for step in range(2):
        for own, target in ((at_top, top_edge), (at_low, low_edge)):

            @pl.when(own)
            def _(step=step, target=target):
                each_other(lambda band: edge_copy(step, band, target).wait_send())

        for own, source, to_top in ((at_top, even_columns, True), (at_low, odd_columns, False)):

            @pl.when(jnp.logical_not(own))
            def _(step=step, source=source, to_top=to_top):
                column_copy(step, source, me, to_top).wait_send()

        upward, downward = row_copies(step)
        upward.wait_send()
        downward.wait_send()


def transport(concentration, emissions, courant):
    bands = lax.axis_size("space")
    _, levels, faces, rows, width = concentration.shape
    held = -(-rows // 8) * 8
    tall = -(-(rows + 6) // 8) * 8
    full = width + 128
    slots = 128 // levels
    f32 = jnp.float32
    vmem = pl.BlockSpec(memory_space=pltpu.VMEM)
    return pl.pallas_call(
        functools.partial(transport_kernel, bands),
        out_shape=(
            jax.ShapeDtypeStruct(concentration.shape, f32),
            jax.ShapeDtypeStruct((faces * rows * (width // 128) * levels, 128), f32),
        ),
        in_specs=[vmem] * 3,
        out_specs=(vmem, vmem),
        scratch_shapes=[
            pltpu.VMEM((levels, faces, tall, full), f32),
            pltpu.VMEM((levels, faces, held, full), f32),
            pltpu.VMEM((levels, faces, tall, width), f32),
            pltpu.VMEM((levels, slots, width), f32),
            pltpu.VMEM((2, bands, held, 128), f32),
            pltpu.VMEM((2, held, 128), f32),
            pltpu.VMEM((2, held, 128), f32),
            pltpu.VMEM((2, held, 128), f32),
            pltpu.VMEM((2, held, 128), f32),
            pltpu.VMEM((2, bands, held, 128), f32),
            pltpu.VMEM((levels, slots, width), f32),
            pltpu.VMEM((2, levels, 24, width), f32),
            pltpu.VMEM((2, levels, 24, width), f32),
            pltpu.VMEM((2, levels, 24, width), f32),
            pltpu.VMEM((2, levels, 24, width), f32),
            pltpu.SemaphoreType.DMA((2, bands)),
            pltpu.SemaphoreType.DMA((2, 2)),
            pltpu.SemaphoreType.DMA((2, 2)),
            pltpu.SemaphoreType.DMA((2, bands)),
            pltpu.SemaphoreType.DMA((2, 2)),
            pltpu.SemaphoreType.DMA((2, 2)),
        ],
        compiler_params=pltpu.CompilerParams(
            collective_id=0, has_side_effects=True, vmem_limit_bytes=52 * 1024 * 1024
        ),
    )(concentration, emissions, courant)


def largest_divisor(number, limit):
    return max(d for d in range(1, limit + 1) if number % d == 0)


def regrid_kernel(rows, chunk, group, source_ref, target_ref, block_ref, weight_ref, sum_ref):
    step = pl.program_id(0)

    @pl.when(step == 0)
    def _():
        sum_ref[...] = jnp.zeros_like(sum_ref)

    def body(index, carry):
        products = []
        for member in range(group):
            local_tile = index * group + member
            source = source_ref[step * chunk + local_tile]
            cells = block_ref[pl.ds(pl.multiple_of(source * rows, rows), rows), :]
            products.append(
                jnp.dot(
                    cells.astype(jnp.bfloat16),
                    weight_ref[local_tile],
                    preferred_element_type=jnp.float32,
                )
            )
        for member in range(group):
            target = target_ref[step * chunk + index * group + member]
            place = pl.ds(pl.multiple_of(target * rows, rows), rows)
            sum_ref[place, :] = sum_ref[place, :] + products[member]
        return carry

    lax.fori_loop(0, chunk // group, body, 0)


def regrid(tile_source, tile_target, blocks, intersection, rows, targets):
    tiles, cells = intersection.shape[0], intersection.shape[1]
    chunk = largest_divisor(tiles, 60)
    group = largest_divisor(chunk, 20)
    summed = pl.pallas_call(
        functools.partial(regrid_kernel, rows, chunk, group),
        grid=(tiles // chunk,),
        out_shape=jax.ShapeDtypeStruct((targets * rows, cells), jnp.float32),
        in_specs=[
            pl.BlockSpec(memory_space=pltpu.SMEM),
            pl.BlockSpec(memory_space=pltpu.SMEM),
            pl.BlockSpec(memory_space=pltpu.VMEM),
            pl.BlockSpec((chunk, cells, cells), lambda step: (step, 0, 0)),
        ],
        out_specs=pl.BlockSpec(memory_space=pltpu.VMEM),
        compiler_params=pltpu.CompilerParams(vmem_limit_bytes=40 * 1024 * 1024),
        cost_estimate=pl.CostEstimate(
            flops=2 * tiles * rows * cells * cells,
            bytes_accessed=2 * tiles * cells * cells,
            transcendentals=0,
        ),
    )(tile_source, tile_target, blocks, intersection)
    return summed.reshape(targets, rows, cells)


def local(concentration, emissions, courant, tile_source, tile_target, intersection):
    band_count = lax.axis_size("space")
    tracer, blocks = transport(concentration, emissions, courant)
    scenarios = tracer.shape[0]
    levels = tracer.shape[1]
    batch_rows = scenarios * levels
    block_cells = intersection.shape[1]
    band_sums = regrid(
        tile_source, tile_target, blocks, intersection, batch_rows, TGT_DEV * band_count
    )
    summed = lax.psum_scatter(
        band_sums,
        "space",
        scatter_dimension=0,
        tiled=True,
    )
    band_result = jnp.swapaxes(summed, 0, 1)
    regridded = band_result.reshape(scenarios, levels, TGT_DEV, block_cells)
    moment_sums = jnp.stack([jnp.sum(regridded, 0), jnp.sum(regridded * regridded, 0)])
    summed_moments = lax.psum(moment_sums, "scen")
    ensemble_moments = summed_moments / (scenarios * lax.axis_size("scen"))
    return (tracer, regridded, ensemble_moments)


def solution(mesh):
    return jax.shard_map(
        local,
        mesh=mesh,
        in_specs=(
            P("scen", None, None, "space", None),
            P("scen", None, "space", None),
            P(None, None, None, "space", None),
            P("space"),
            P("space"),
            P("space", None, None),
        ),
        out_specs=(
            P("scen", None, None, "space", None),
            P("scen", None, "space", None),
            P(None, None, "space", None),
        ),
        check_vma=False,
    )
```

profile of v0, /device:TPU:10, one launch (start us, length us, event | category | flops | bytes accessed | tf_op | source)
XLA Modules:
  0.0 192.7 jit_solution(203034682081259922)
XLA Ops:
  7.2 0.0 reduce-scatter.2.cloned.1.call-start
  7.2 0.0 copy-start.1
  7.2 0.9 copy-done.1
  8.1 0.0 copy-start.2
  8.2 0.0 copy-start.3
  8.2 69.0 %shard_map.85 = (f32[1,8,6,24,384]{4,3,2,1,0:T(8,128)S(1)}, f32[3456,128]{1,0:T(8,128)}) custom-call(f32[1,8,6,24,384]{4,3,2,1,0:T(8,128)} %conc_ref.1, f32[1,6,24,384]{3,2,1,0:T(8,128)S(1)} %copy-done.1, f32[2,8,6,24,384]{4,3,2,1,0:T(8,128)} %wind_ref.1), custom_call_target="tpu_custom_call" | custom-call | tf_op jit(solution)/shard_map/pallas_call | solution.py:381
  77.2 0.0 copy-done.2
  77.2 0.0 copy-done.3
  77.2 0.0 copy-start
  77.2 1.5 copy-done
  78.7 12.4 %shard_map.86 = f32[4096,128]{1,0:T(8,128)S(1)} custom-call(s32[540]{0:T(1024)S(1)} %copy-done.2, s32[540]{0:T(1024)S(1)} %copy-done.3, f32[3456,128]{1,0:T(8,128)S(1)} %copy-done, bf16[540,128,128]{2,1,0:T(8,128)(2,1)} %weight_ref.1), custom_call_target="tpu_custom_call" | custom-call | flops 141557760 | bytes 17694720 | tf_op jit(solution)/shard_map/pallas_call | solution.py:455
  91.1 1.7 copy.9
  92.8 0.0 reduce-scatter.2.cloned.1.call-update
  92.9 0.0 all-reduce.2.cloned.1.call-start
  92.9 64.7 %reduce-scatter.2.cloned.1.call-done = f32[32,8,128]{2,0,1:T(8,128)} async-done(((f32[512,8,128]{2,0,1:T(8,128)}), f32[32,8,128]{2,0,1:T(8,128)}) %reduce-scatter.2.cloned.1.call-update) | async-done | bytes 131088 | tf_op jit(solution)/shard_map/reduce_scatter | solution.py:486
  157.6 0.9 fusion
  158.5 1.6 pad_maximum_fusion
  160.2 0.0 all-reduce.2.cloned.1.call-update
  160.2 22.8 %all-reduce.2.cloned.1.call-done = f32[2,8,32,128]{3,2,1,0:T(8,128)} async-done(((f32[2,8,32,128]{3,2,1,0:T(8,128)}), f32[2,8,32,128]{3,2,1,0:T(8,128)}) %all-reduce.2.cloned.1.call-update) | async-done | bytes 262160 | tf_op jit(solution)/shard_map/psum | solution.py:495
  183.0 1.7 broadcast_multiply_fusion
  184.6 1.2 copy.12
Async XLA Ops:
  7.2 150.5 %reduce-scatter.2.cloned.1.call-start = ((), (), s32[]{:S(2)}) async-start(), calls=%async_computation.1 | async-start | bytes 2228224 | tf_op jit(solution)/shard_map/reduce_scatter | solution.py:486
  7.2 0.9 copy-start.1
  8.1 69.0 %copy-start.2 = (s32[540]{0:T(1024)S(1)}, s32[540]{0:T(1024)}, u32[]{:S(2)}) copy-start(s32[540]{0:T(1024)} %source_ref.1) | copy-start | bytes 6484
  8.2 69.0 %copy-start.3 = (s32[540]{0:T(1024)S(1)}, s32[540]{0:T(1024)}, u32[]{:S(2)}) copy-start(s32[540]{0:T(1024)} %target_ref.1) | copy-start | bytes 6484
  77.2 1.5 copy-start
  92.9 90.1 %all-reduce.2.cloned.1.call-start = ((), (), s32[]{:S(2)}) async-start(), calls=%async_computation.2 | async-start | bytes 524288 | tf_op jit(solution)/shard_map/psum | solution.py:495
Sparse Core Ops, SparseCore 0:
  93.0 64.6 reduce-scatter.1
  160.6 22.3 all-reduce.1
where the time goes:
time: 195 us; the launch traced here: 193 us
  waiting for transfers between devices  87.5 us (45%)
  Pallas kernels  81.4 us (42%)
  between operations  14.1 us (7%)
  local copies, waits for them, and re-layouts  5.33 us (3%)
  other arithmetic  4.22 us (2%)
    pallas_call x1, Pallas kernels, transport(): pl.pallas_call(functools.partial(transport_kernel, bands), out_shape=(jax...  69 us
    reduce_scatter x1, waiting for transfers between devices, local(): lax.psum_scatter(band_sums, 'space', scatter_dimension=0, tiled=True)  64.7 us
    psum x1, waiting for transfers between devices, local(): summed_moments = lax.psum(moment_sums, 'scen')  22.8 us
    pallas_call x1, Pallas kernels, regrid(): pl.pallas_call(functools.partial(regrid_kernel, rows, chunk, group), grid...  12.4 us
  transfers between devices with their start and end apart: 2, of which 2 were waited for; matrix products, arithmetic and copies ran while one was open for 0% of the time, Pallas kernels for 0%

commit v1 on v0

--- a/solution.py
+++ b/solution.py
@@ -473,6 +473,162 @@
     return summed.reshape(targets, rows, cells)
 
 
+def combine_kernel(
+    scenarios,
+    part_ref,
+    regrid_ref,
+    moment_ref,
+    core_in,
+    pair_sum,
+    side_in,
+    side_sum,
+    far_in,
+    mine,
+    ensemble,
+    core_send,
+    core_recv,
+    side_send,
+    side_recv,
+    far_send,
+    far_recv,
+    scen_send,
+    scen_recv,
+):
+    me = lax.axis_index("space")
+    scen = lax.axis_index("scen")
+    layers = part_ref.shape[0]
+    levels, blocks = regrid_ref.shape[0], regrid_ref.shape[1]
+    core, side, layer = lax.rem(me, 2), lax.rem(me // 2, 2), me // 4
+    sibling = {"space": me + 1 - 2 * core}
+    beside = {"space": me + 2 - 4 * side}
+
+    def far_device(other):
+        return {"space": other * 4 + side * 2 + core}
+
+    def ahead(step):
+        return lax.rem(layer + step, layers)
+
+    def other_scen(step):
+        return lax.rem(scen + step, scenarios)
+
+    barrier = pltpu.get_barrier_semaphore()
+    peers = [sibling, beside]
+    peers += [far_device(ahead(step)) for step in range(1, layers)]
+    peers += [{"scen": other_scen(step)} for step in range(1, scenarios)]
+    for peer in peers:
+        pl.semaphore_signal(barrier, inc=1, device_id=peer, device_id_type=MESH)
+    pl.semaphore_wait(barrier, len(peers))
+
+    def remote(source, target, send_sem, recv_sem, device):
+        return pltpu.make_async_remote_copy(
+            src_ref=source,
+            dst_ref=target,
+            send_sem=send_sem,
+            recv_sem=recv_sem,
+            device_id=device,
+            device_id_type=MESH,
+        )
+
+    def core_copy(at):
+        return remote(
+            part_ref.at[at, :, 1 - core], core_in.at[at], core_send.at[at], core_recv.at[at], sibling
+        )
+
+    def side_copy(at):
+        return remote(
+            pair_sum.at[at, 1 - side], side_in.at[at], side_send.at[at], side_recv.at[at], beside
+        )
+
+    def far_copy(at):
+        return remote(
+            side_sum.at[at], far_in.at[layer], far_send.at[at], far_recv.at[layer], far_device(at)
+        )
+
+    def far_arrival(at):
+        return remote(
+            side_sum.at[at], far_in.at[at], far_send.at[at], far_recv.at[at], far_device(at)
+        )
+
+    def scen_copy(to, slot):
+        return remote(mine, ensemble.at[slot], scen_send.at[to], scen_recv.at[slot], {"scen": to})
+
+    order = [ahead(step) for step in range(1, layers + 1)]
+    for at in order:
+        core_copy(at).start()
+    for at in order:
+        core_copy(at).wait_recv()
+        pair_sum[at, 1 - side] = part_ref[at, 1 - side, core] + core_in[at, 1 - side]
+        side_copy(at).start()
+        pair_sum[at, side] = part_ref[at, side, core] + core_in[at, side]
+    for at in order:
+        side_copy(at).wait_recv()
+        side_sum[at] = pair_sum[at, side] + side_in[at]
+        if at is not order[-1]:
+            far_copy(at).start()
+    mine[...] = side_sum[layer]
+    for at in order[:-1]:
+        far_arrival(at).wait_recv()
+        mine[...] = mine[...] + far_in[at]
+    for step in range(1, scenarios):
+        scen_copy(other_scen(step), scen).start()
+    ensemble[scen] = mine[...]
+    for level in range(levels):
+        regrid_ref[level] = mine[pl.ds(level, blocks, stride=levels), :]
+    for step in range(1, scenarios):
+        scen_copy(other_scen(step), other_scen(step)).wait_recv()
+    mean = ensemble[0]
+    square = mean * mean
+    for index in range(1, scenarios):
+        member = ensemble[index]
+        mean = mean + member
+        square = square + member * member
+    far_in[0] = mean / scenarios
+    side_in[0] = square / scenarios
+    for level in range(levels):
+        moment_ref[0, level] = far_in[0, pl.ds(level, blocks, stride=levels), :]
+        moment_ref[1, level] = side_in[0, pl.ds(level, blocks, stride=levels), :]
+    for at in order:
+        core_copy(at).wait_send()
+        side_copy(at).wait_send()
+        if at is not order[-1]:
+            far_copy(at).wait_send()
+    for step in range(1, scenarios):
+        scen_copy(other_scen(step), scen).wait_send()
+
+
+def combine(band_sums, levels):
+    bands, scenarios = lax.axis_size("space"), lax.axis_size("scen")
+    cells = band_sums.shape[-1]
+    layers = bands // 4
+    held = TGT_DEV * levels
+    f32 = jnp.float32
+    vmem = pl.BlockSpec(memory_space=pltpu.VMEM)
+    parts = band_sums.reshape(layers, 2, 2, held, cells)
+    return pl.pallas_call(
+        functools.partial(combine_kernel, scenarios),
+        out_shape=(
+            jax.ShapeDtypeStruct((levels, TGT_DEV, cells), f32),
+            jax.ShapeDtypeStruct((2, levels, TGT_DEV, cells), f32),
+        ),
+        in_specs=[vmem],
+        out_specs=(vmem, vmem),
+        scratch_shapes=[
+            pltpu.VMEM((layers, 2, held, cells), f32),
+            pltpu.VMEM((layers, 2, held, cells), f32),
+            pltpu.VMEM((layers, held, cells), f32),
+            pltpu.VMEM((layers, held, cells), f32),
+            pltpu.VMEM((layers, held, cells), f32),
+            pltpu.VMEM((held, cells), f32),
+            pltpu.VMEM((scenarios, held, cells), f32),
+        ]
+        + [pltpu.SemaphoreType.DMA((layers,))] * 6
+        + [pltpu.SemaphoreType.DMA((scenarios,))] * 2,
+        compiler_params=pltpu.CompilerParams(
+            collective_id=1, has_side_effects=True, vmem_limit_bytes=48 * 1024 * 1024
+        ),
+    )(parts)
+
+
 def local(concentration, emissions, courant, tile_source, tile_target, intersection):
     band_count = lax.axis_size("space")
     tracer, blocks = transport(concentration, emissions, courant)
@@ -483,18 +639,8 @@
     band_sums = regrid(
         tile_source, tile_target, blocks, intersection, batch_rows, TGT_DEV * band_count
     )
-    summed = lax.psum_scatter(
-        band_sums,
-        "space",
-        scatter_dimension=0,
-        tiled=True,
-    )
-    band_result = jnp.swapaxes(summed, 0, 1)
-    regridded = band_result.reshape(scenarios, levels, TGT_DEV, block_cells)
-    moment_sums = jnp.stack([jnp.sum(regridded, 0), jnp.sum(regridded * regridded, 0)])
-    summed_moments = lax.psum(moment_sums, "scen")
-    ensemble_moments = summed_moments / (scenarios * lax.axis_size("scen"))
-    return (tracer, regridded, ensemble_moments)
+    regridded, ensemble_moments = combine(band_sums, levels)
+    return (tracer, regridded[None], ensemble_moments)
 
 
 def solution(mesh):

time: 195 us -> 119 us (0.61)
  waiting for transfers between devices: 87.5 us -> 0 us
  Pallas kernels: 81.4 us -> 113 us
  between operations: 14.1 us -> 0.69 us
  other arithmetic: 4.22 us -> 0 us
    reduce_scatter x1 -> x0, waiting for transfers between devices: 64.7 us -> none  [local(): lax.psum_scatter(band_sums, 'space', scatter_dimension=0, tiled=True)]
    pallas_call x0 -> x1, Pallas kernels: none -> 31.5 us  [combine(): pl.pallas_call(functools.partial(combine_kernel, scenarios), out_shape=(j...]
    psum x1 -> x0, waiting for transfers between devices: 22.8 us -> none  [local(): summed_moments = lax.psum(moment_sums, 'scen')]
    unnamed x9 -> x11, local copies, waits for them, and re-layouts: 3.61 us -> 4.97 us
  transfers between devices with their start and end apart: 2 -> 0, of which waited for: 2 -> 0; matrix products, arithmetic and copies ran while one was open for 0% -> 0% of each run, Pallas kernels for 0% -> 0%
where the time goes in v1:
time: 119 us
  Pallas kernels  113 us (95%)
  local copies, waits for them, and re-layouts  4.97 us (4%)
    pallas_call x1, Pallas kernels, transport(): pl.pallas_call(functools.partial(transport_kernel, bands), out_shape=(jax...  69 us
    pallas_call x1, Pallas kernels, combine(): pl.pallas_call(functools.partial(combine_kernel, scenarios), out_shape=(j...  31.5 us
    pallas_call x1, Pallas kernels, regrid(): pl.pallas_call(functools.partial(regrid_kernel, rows, chunk, group), grid...  12.4 us
    unnamed x11, local copies, waits for them, and re-layouts  4.97 us

profile of v1, /device:TPU:10, one launch (start us, length us, event | category | flops | bytes accessed | tf_op | source)
XLA Modules:
  0.0 118.6 jit_solution(3146316205496031811)
XLA Ops:
  0.6 0.0 copy-start.1
  0.6 0.9 copy-done.1
  1.6 0.0 copy-start.2
  1.6 0.0 copy-start.3
  1.6 69.0 %shard_map.85 = (f32[1,8,6,24,384]{4,3,2,1,0:T(8,128)S(1)}, f32[3456,128]{1,0:T(8,128)}) custom-call(f32[1,8,6,24,384]{4,3,2,1,0:T(8,128)} %conc_ref.1, f32[1,6,24,384]{3,2,1,0:T(8,128)S(1)} %copy-done.1, f32[2,8,6,24,384]{4,3,2,1,0:T(8,128)} %wind_ref.1), custom_call_target="tpu_custom_call" | custom-call | tf_op jit(solution)/shard_map/pallas_call | solution.py:381
  70.6 0.0 copy-done.2
  70.6 0.0 copy-done.3
  70.6 0.0 copy-start
  70.6 1.5 %copy-done = f32[3456,128]{1,0:T(8,128)S(1)} copy-done((f32[3456,128]{1,0:T(8,128)S(1)}, f32[3456,128]{1,0:T(8,128)}, u32[]{:S(2)}) %copy-start) | copy-done | bytes 1769496
  72.1 12.4 %shard_map.86 = f32[4096,128]{1,0:T(8,128)S(1)} custom-call(s32[540]{0:T(1024)S(1)} %copy-done.2, s32[540]{0:T(1024)S(1)} %copy-done.3, f32[3456,128]{1,0:T(8,128)S(1)} %copy-done, bf16[540,128,128]{2,1,0:T(8,128)(2,1)} %weight_ref.1), custom_call_target="tpu_custom_call" | custom-call | flops 141557760 | bytes 17694720 | tf_op jit(solution)/shard_map/pallas_call | solution.py:455
  84.5 31.5 %shard_map.87 = (f32[8,32,128]{2,1,0:T(8,128)S(1)}, f32[2,8,32,128]{3,2,1,0:T(8,128)S(1)}) custom-call(f32[4,2,2,256,128]{4,3,2,1,0:T(8,128)S(1)} %bitcast.2), custom_call_target="tpu_custom_call" | custom-call | tf_op jit(solution)/shard_map/pallas_call | solution.py:607
  116.0 1.2 %copy.12 = f32[1,8,6,24,384]{4,3,2,1,0:T(8,128)} copy(f32[1,8,6,24,384]{4,3,2,1,0:T(8,128)S(1)} %get-tuple-element.14) | data formatting | bytes 3538944
  117.2 0.7 copy.13
  117.9 0.7 copy.14
Async XLA Ops:
  0.6 0.9 copy-start.1
  1.6 69.0 %copy-start.2 = (s32[540]{0:T(1024)S(1)}, s32[540]{0:T(1024)}, u32[]{:S(2)}) copy-start(s32[540]{0:T(1024)} %source_ref.1) | copy-start | bytes 6484
  1.6 69.0 %copy-start.3 = (s32[540]{0:T(1024)S(1)}, s32[540]{0:T(1024)}, u32[]{:S(2)}) copy-start(s32[540]{0:T(1024)} %target_ref.1) | copy-start | bytes 6484
  70.6 1.5 %copy-start = (f32[3456,128]{1,0:T(8,128)S(1)}, f32[3456,128]{1,0:T(8,128)}, u32[]{:S(2)}) copy-start(f32[3456,128]{1,0:T(8,128)} %get-tuple-element.8.block_ref) | copy-start | bytes 5308420

commit v2 on v1

--- a/solution.py
+++ b/solution.py
@@ -120,20 +120,20 @@
             device_id_type=MESH,
         )
 
-    def row_copies(step):
+    def row_copies(step, level):
         upward = pltpu.make_async_remote_copy(
-            src_ref=rows_up.at[step],
-            dst_ref=from_south.at[step],
-            send_sem=row_send.at[step, 0],
-            recv_sem=row_recv.at[step, 0],
+            src_ref=rows_up.at[step, level],
+            dst_ref=from_south.at[step, level],
+            send_sem=row_send.at[step, 0, level],
+            recv_sem=row_recv.at[step, 0, level],
             device_id={"space": lax.rem(me + 1, bands)},
             device_id_type=MESH,
         )
         downward = pltpu.make_async_remote_copy(
-            src_ref=rows_down.at[step],
-            dst_ref=from_north.at[step],
-            send_sem=row_send.at[step, 1],
-            recv_sem=row_recv.at[step, 1],
+            src_ref=rows_down.at[step, level],
+            dst_ref=from_north.at[step, level],
+            send_sem=row_send.at[step, 1, level],
+            recv_sem=row_recv.at[step, 1, level],
             device_id={"space": lax.rem(me + bands - 1, bands)},
             device_id_type=MESH,
         )
@@ -260,13 +260,13 @@
                         odd_columns[step, 0:rows] = odd_columns[step, 0:rows] + moved(
                             edge, 127, base
                         )
+            upward, downward = row_copies(step, level)
+            upward.start()
+            downward.start()
             return carry
 
         lax.fori_loop(0, levels, sweep_east, 0)
 
-        upward, downward = row_copies(step)
-        upward.start()
-        downward.start()
         for own, source, to_top in ((at_top, even_columns, True), (at_low, odd_columns, False)):
 
             @pl.when(jnp.logical_not(own))
@@ -287,10 +287,10 @@
                 )
                 turned[...] = result.reshape(levels, slots, width)
 
-        upward.wait_recv()
-        downward.wait_recv()
-
         def sweep_north(level, carry, step=step):
+            upward, downward = row_copies(step, level)
+            upward.wait_recv()
+            downward.wait_recv()
             for face in range(6):
                 north_face, south_face = face, face
                 if face % 2 == 0:
@@ -364,9 +364,13 @@
             def _(step=step, source=source, to_top=to_top):
                 column_copy(step, source, me, to_top).wait_send()
 
-        upward, downward = row_copies(step)
-        upward.wait_send()
-        downward.wait_send()
+        def sent(level, carry, step=step):
+            upward, downward = row_copies(step, level)
+            upward.wait_send()
+            downward.wait_send()
+            return carry
+
+        lax.fori_loop(0, levels, sent, 0)
 
 
 def transport(concentration, emissions, courant):
@@ -406,8 +410,8 @@
             pltpu.SemaphoreType.DMA((2, 2)),
             pltpu.SemaphoreType.DMA((2, 2)),
             pltpu.SemaphoreType.DMA((2, bands)),
-            pltpu.SemaphoreType.DMA((2, 2)),
-            pltpu.SemaphoreType.DMA((2, 2)),
+            pltpu.SemaphoreType.DMA((2, 2, levels)),
+            pltpu.SemaphoreType.DMA((2, 2, levels)),
         ],
         compiler_params=pltpu.CompilerParams(
             collective_id=0, has_side_effects=True, vmem_limit_bytes=52 * 1024 * 1024

time: 119 us -> 111 us (0.933)
  Pallas kernels: 113 us -> 105 us
    pallas_call x1, Pallas kernels: 69 us -> 57.5 us  [transport(): pl.pallas_call(functools.partial(transport_kernel, bands), out_shape=(jax...]
    pallas_call x1, Pallas kernels: 31.5 us -> 34.9 us  [combine(): pl.pallas_call(functools.partial(combine_kernel, scenarios), out_shape=(j...]
where the time goes in v2:
time: 111 us; the launch traced here: 110 us
  Pallas kernels  105 us (95%)
  local copies, waits for them, and re-layouts  4.97 us (4%)
    pallas_call x1, Pallas kernels, transport(): pl.pallas_call(functools.partial(transport_kernel, bands), out_shape=(jax...  57.5 us
    pallas_call x1, Pallas kernels, combine(): pl.pallas_call(functools.partial(combine_kernel, scenarios), out_shape=(j...  34.9 us
    pallas_call x1, Pallas kernels, regrid(): pl.pallas_call(functools.partial(regrid_kernel, rows, chunk, group), grid...  12.4 us
    unnamed x11, local copies, waits for them, and re-layouts  4.97 us

profile of v2, /device:TPU:10, one launch (start us, length us, event | category | flops | bytes accessed | tf_op | source)
XLA Modules:
  0.0 110.5 jit_solution(10816060301055179132)
XLA Ops:
  0.6 0.0 copy-start.1
  0.6 0.9 copy-done.1
  1.6 0.0 copy-start.2
  1.6 0.0 copy-start.3
  1.6 57.5 %shard_map.85 = (f32[1,8,6,24,384]{4,3,2,1,0:T(8,128)S(1)}, f32[3456,128]{1,0:T(8,128)}) custom-call(f32[1,8,6,24,384]{4,3,2,1,0:T(8,128)} %conc_ref.1, f32[1,6,24,384]{3,2,1,0:T(8,128)S(1)} %copy-done.1, f32[2,8,6,24,384]{4,3,2,1,0:T(8,128)} %wind_ref.1), custom_call_target="tpu_custom_call" | custom-call | tf_op jit(solution)/shard_map/pallas_call | solution.py:385
  59.0 0.0 copy-done.2
  59.1 0.0 copy-done.3
  59.1 0.0 copy-start
  59.1 1.5 %copy-done = f32[3456,128]{1,0:T(8,128)S(1)} copy-done((f32[3456,128]{1,0:T(8,128)S(1)}, f32[3456,128]{1,0:T(8,128)}, u32[]{:S(2)}) %copy-start) | copy-done | bytes 1769496
  60.5 12.4 %shard_map.86 = f32[4096,128]{1,0:T(8,128)S(1)} custom-call(s32[540]{0:T(1024)S(1)} %copy-done.2, s32[540]{0:T(1024)S(1)} %copy-done.3, f32[3456,128]{1,0:T(8,128)S(1)} %copy-done, bf16[540,128,128]{2,1,0:T(8,128)(2,1)} %weight_ref.1), custom_call_target="tpu_custom_call" | custom-call | flops 141557760 | bytes 17694720 | tf_op jit(solution)/shard_map/pallas_call | solution.py:459
  73.0 34.9 %shard_map.87 = (f32[8,32,128]{2,1,0:T(8,128)S(1)}, f32[2,8,32,128]{3,2,1,0:T(8,128)S(1)}) custom-call(f32[4,2,2,256,128]{4,3,2,1,0:T(8,128)S(1)} %bitcast.2), custom_call_target="tpu_custom_call" | custom-call | tf_op jit(solution)/shard_map/pallas_call | solution.py:611
  107.9 1.2 %copy.12 = f32[1,8,6,24,384]{4,3,2,1,0:T(8,128)} copy(f32[1,8,6,24,384]{4,3,2,1,0:T(8,128)S(1)} %get-tuple-element.14) | data formatting | bytes 3538944
  109.1 0.7 copy.13
  109.8 0.7 copy.14
Async XLA Ops:
  0.6 0.9 copy-start.1
  1.6 57.5 %copy-start.2 = (s32[540]{0:T(1024)S(1)}, s32[540]{0:T(1024)}, u32[]{:S(2)}) copy-start(s32[540]{0:T(1024)} %source_ref.1) | copy-start | bytes 6484
  1.6 57.5 %copy-start.3 = (s32[540]{0:T(1024)S(1)}, s32[540]{0:T(1024)}, u32[]{:S(2)}) copy-start(s32[540]{0:T(1024)} %target_ref.1) | copy-start | bytes 6484
  59.1 1.5 %copy-start = (f32[3456,128]{1,0:T(8,128)S(1)}, f32[3456,128]{1,0:T(8,128)}, u32[]{:S(2)}) copy-start(f32[3456,128]{1,0:T(8,128)} %get-tuple-element.8.block_ref) | copy-start | bytes 5308420
